TPU v7x, 32 devices: a whole 2x2x4 slice. The times are simulated.
32 devices in a mesh: seq: 8 (over z, x), type: 4 (over y, core).
Axes of the slice: x: 2, y: 2, z: 4, core: 2. Of those that a mesh axis runs over, the one named last changes fastest.
Arguments:
- tokens: bfloat16 [4352, 1024], P(('seq', 'type')), may hold values from -60 to 60
- shift_scale: float32 [2, 1024], replicated, may hold values from -0.8 to 0.8
- branch_gate: float32 [1024], replicated, may hold values from 0.25 to 1.75
- final_gain: float32 [1024], replicated, may hold values from 0.5 to 1.5
- w_qkv: bfloat16 [3, 1024, 1024], P(None, None, 'type'), may hold values from -1 to 1
- w_out: bfloat16 [1024, 1024], P('type'), may hold values from -0.375 to 0.375
- type_ids: int32 [4352, 1], P(('seq', 'type')), may hold values from 0 to 7; in each aligned block of 136 rows (0 to 135, 136 to 271, ...) at most 51 rows name the same one
- head_w1: bfloat16 [8, 1024, 1024], P('type'), may hold values from -0.1875 to 0.1875
- head_b1: bfloat16 [8, 1024], P('type'), may hold values from -3 to 3
- head_w2: bfloat16 [8, 1024, 16], P('type'), may hold values from -0.1875 to 0.1875
Outputs:
- updated: bfloat16 [4352, 1024], P(('seq', 'type'))
- head_out: float32 [4352, 16], P(('seq', 'type'))
Inputs may be any that keep to these rules, and one draw needn't show every extreme that they name: `type_ids`: among the 136 tokens of one device no type occurs more than 51 times; some type occurs exactly 51 times on some devices.
All inputs are finite; a program needn't handle non-finite values.
Results may differ from a plain program's by a relative error of at most 0.014.
Values may be sent and summed in bfloat16 or wider, within the bound.
A program may use at most 192 MiB of HBM per device.

v0:
```python
import jax
import jax.numpy as jnp
from jax import lax
from jax.sharding import PartitionSpec as P

HD = 64


def rms_normalize(values):
    squares = jnp.mean(values * values, axis=-1, keepdims=True)
    return values * lax.rsqrt(squares + 1e-06)


def absorb_block(state, query_heads, key_heads, value_heads):
    largest, totals, numer = state
    scores = jnp.einsum(
        "qhd,khd->hqk", query_heads, key_heads, preferred_element_type=jnp.float32
    ) * HD ** (-0.5)
    newmax = jnp.maximum(largest, jnp.max(scores, axis=-1))
    decay = jnp.exp(largest - newmax)
    weights = jnp.exp(scores - newmax[:, :, None])
    totals = totals * decay + jnp.sum(weights, axis=-1)
    update = jnp.einsum(
        "hqk,khd->qhd",
        weights.astype(jnp.bfloat16),
        value_heads,
        preferred_element_type=jnp.float32,
    )
    numer = numer * jnp.transpose(decay)[:, :, None] + update
    return (newmax, totals, numer)


def apply_heads(feature_slots, first_w, first_b, second_w):
    hidden = jnp.einsum(
        "...tcd,tdh->...tch", feature_slots, first_w, preferred_element_type=jnp.float32
    )
    hidden = jax.nn.gelu(hidden + first_b.astype(jnp.float32)[:, None, :]).astype(jnp.bfloat16)
    return jnp.einsum("...tch,tho->...tco", hidden, second_w, preferred_element_type=jnp.float32)


def body(
    tokens, shift_scale, branch_gate, final_gain, w_qkv, w_out, type_ids, head_w1, head_b1, head_w2
):
    inputs = tokens.astype(jnp.float32)
    modulated = (rms_normalize(inputs) * (1.0 + shift_scale[1]) + shift_scale[0]).astype(
        jnp.bfloat16
    )
    projected = jnp.einsum(
        "rd,ide->ire",
        lax.all_gather(modulated, "type", axis=0, tiled=True),
        w_qkv,
        preferred_element_type=jnp.float32,
    ).astype(jnp.bfloat16)
    queries = projected[0]
    local_keys = projected[1]
    local_values = projected[2]
    query_count = queries.shape[0]
    width = queries.shape[1]
    local_heads = width // HD
    query_heads = queries.reshape(query_count, local_heads, HD)
    initial = (
        jnp.full((local_heads, query_count), -1e30, jnp.float32),
        jnp.zeros((local_heads, query_count), jnp.float32),
        jnp.zeros((query_count, local_heads, HD), jnp.float32),
    )

    def absorb(running, key_value):
        key_part, value_part = key_value
        row_total = key_part.shape[0]
        if row_total > 512 and row_total % 512 == 0:
            key_blocks = key_part.reshape(row_total // 512, 512, local_heads, HD)
            value_blocks = value_part.reshape(row_total // 512, 512, local_heads, HD)

            def advance(state, pair):
                return (absorb_block(state, query_heads, pair[0], pair[1]), None)

            running, unused = lax.scan(advance, running, (key_blocks, value_blocks))
            return running
        return absorb_block(
            running,
            query_heads,
            key_part.reshape(row_total, local_heads, HD),
            value_part.reshape(row_total, local_heads, HD),
        )

    largest, totals, numer = absorb(
        initial,
        (
            lax.all_gather(local_keys, "seq", axis=0, tiled=True),
            lax.all_gather(local_values, "seq", axis=0, tiled=True),
        ),
    )
    attended = (
        (numer / jnp.transpose(totals)[:, :, None]).astype(jnp.bfloat16).reshape(query_count, width)
    )
    mixed = lax.psum_scatter(
        jnp.dot(attended, w_out, preferred_element_type=jnp.float32),
        "type",
        scatter_dimension=0,
        tiled=True,
    )
    updated = (inputs + branch_gate * mixed).astype(jnp.bfloat16)
    final = (rms_normalize(updated.astype(jnp.float32)) * final_gain).astype(jnp.bfloat16)
    owned = head_w1.shape[0]
    owners = lax.axis_size("type")
    kinds_all = owned * owners
    capacity = 3 * tokens.shape[0] // 8
    kinds = type_ids[:, 0]
    onehot = (kinds[:, None] == jnp.arange(kinds_all, dtype=jnp.int32)[None, :]).astype(jnp.int32)
    ranks = jnp.sum((jnp.cumsum(onehot, axis=0) - onehot) * onehot, axis=1)
    slots = kinds * capacity + ranks
    slot_ids = jnp.arange(kinds_all * capacity, dtype=jnp.int32)
    dispatch = (slot_ids[:, None] == slots[None, :]).astype(jnp.bfloat16)
    packed = jnp.dot(dispatch, final, preferred_element_type=jnp.float32).astype(jnp.bfloat16)
    packed = packed.reshape(kinds_all, capacity, final.shape[1])
    first_w, first_b, second_w = (
        lax.all_gather(head_w1, "type", axis=0, tiled=True),
        lax.all_gather(head_b1, "type", axis=0, tiled=True),
        lax.all_gather(head_w2, "type", axis=0, tiled=True),
    )
    answers = apply_heads(packed, first_w, first_b, second_w)
    answers = answers.reshape(kinds_all * capacity, head_w2.shape[2])
    gather_back = (slots[:, None] == slot_ids[None, :]).astype(jnp.float32)
    head_out = jnp.dot(
        gather_back, answers, precision=lax.Precision.HIGHEST, preferred_element_type=jnp.float32
    )
    return (updated, head_out)


def solution(mesh):
    in_specs = (
        P(("seq", "type"), None),
        P(),
        P(),
        P(),
        P(None, None, "type"),
        P("type", None),
        P(("seq", "type"), None),
        P("type", None, None),
        P("type", None),
        P("type", None, None),
    )
    out_specs = (P(("seq", "type"), None), P(("seq", "type"), None))
    return jax.shard_map(body, mesh=mesh, in_specs=in_specs, out_specs=out_specs, check_vma=False)
```

profile of v0, /device:TPU:0, one launch (start us, length us, event | category | flops | bytes accessed | tf_op | source)
XLA Modules:
  0.0 311.8 jit_solution(2549402294202756651)
XLA Ops:
  7.2 0.0 copy-start
  7.2 0.0 all-gather.8.cloned.1.call-start
  7.2 0.8 slice_add_fusion
  8.1 1.1 fusion.35
  9.2 1.8 fusion.38
  11.0 0.0 all-gather.8.cloned.1.call-update
  11.0 0.0 all-gather.12.cloned.1.call-start
  11.1 19.9 %all-gather.8.cloned.1.call-done = bf16[544,1024]{1,0:T(8,128)(2,1)} async-done(((bf16[136,1024]{1,0:T(8,128)(2,1)}), bf16[544,1024]{1,0:T(8,128)(2,1)}) %all-gather.8.cloned.1.call-update) | async-done | bytes 1114128 | tf_op jit(solution)/shard_map/all_gather | solution.py:50
  31.0 2.3 fusion.12
  33.2 0.8 fusion.54
  34.1 0.0 all-gather.12.cloned.1.call-update
  34.1 0.0 all-gather.14.cloned.1.call-start
  34.2 0.2 copy.19
  34.4 0.5 all-gather.14.cloned.1.call-update
  34.9 0.0 reduce-scatter.2.cloned.1.call-start
  34.9 50.0 %all-gather.12.cloned.1.call-done = bf16[1,4352,256]{2,1,0:T(8,128)(2,1)} async-done(((bf16[1,544,256]{2,1,0:T(8,128)(2,1)}), bf16[1,4352,256]{2,1,0:T(8,128)(2,1)}) %all-gather.12.cloned.1.call-update) | async-done | bytes 2228240 | tf_op jit(solution)/shard_map/all_gather | solution.py:89
  84.9 4.1 %copy.20 = bf16[1,4352,256]{1,2,0:T(8,128)(2,1)} copy(bf16[1,4352,256]{2,1,0:T(8,128)(2,1)} %all-gather.12.cloned.1.call-done) | data formatting | bytes 4456448 | tf_op jit(solution)/shard_map/all_gather | solution.py:89
  89.1 16.1 %multiply_reduce_fusion = (f32[4,544]{1,0:T(4,128)S(1)}, f32[4,544,4352]{2,1,0:T(8,128)}) fusion(bf16[544,4,64]{0,2,1:T(8,128)(2,1)S(1)} %bitcast.50, bf16[4352,4,64]{0,2,1:T(8,128)(2,1)} %bitcast.48), kind=kOutput, calls=%fused_computation.1 | convolution fusion | flops 1231091584 | bytes 40395264 | tf_op jit(solution)/shard_map/qhd,khd->hqk/dot_general | solution.py:16
  105.2 16.8 %fusion = f32[4,544]{1,0:T(4,128)S(1)} fusion(f32[4,544,4352]{2,1,0:T(8,128)} %get-tuple-element.12, f32[4,544]{1,0:T(4,128)S(1)} %get-tuple-element.8), kind=kLoop, calls=%fused_computation.2 | loop fusion | flops 28407680 | bytes 37897216 | tf_op jit(solution)/shard_map/reduce_sum | solution.py:22
  122.0 14.3 %all-gather.14.cloned.1.call-done = bf16[1,4352,256]{2,1,0:T(8,128)(2,1)} async-done(((bf16[1,544,256]{2,1,0:T(8,128)(2,1)}), bf16[1,4352,256]{2,1,0:T(8,128)(2,1)}) %all-gather.14.cloned.1.call-update) | async-done | bytes 2228240 | tf_op jit(solution)/shard_map/all_gather | solution.py:90
  136.3 4.1 %copy.21 = bf16[1,4352,256]{1,2,0:T(8,128)(2,1)} copy(bf16[1,4352,256]{2,1,0:T(8,128)(2,1)} %all-gather.14.cloned.1.call-done) | data formatting | bytes 4456448 | tf_op jit(solution)/shard_map/all_gather | solution.py:90
  140.5 15.9 %fusion.23 = bf16[544,4,64]{0,2,1:T(8,128)(2,1)S(1)} fusion(bf16[4352,4,64]{0,2,1:T(8,128)(2,1)} %bitcast.47, f32[4,544,4352]{2,1,0:T(8,128)} %get-tuple-element.12, f32[4,544]{1,0:T(4,128)S(1)} %get-tuple-element.8, f32[544,4]{0,1:T(4,128)S(1)} %bitcast_add_fusion, f32[544,4]{0,1:T(4,128)S(1)} %get-tuple-element.7), kind=kOutput, calls=%fused_computation.21 | convolution fusion | flops 1240981504 | bytes 40412672 | tf_op jit(solution)/shard_map/hqk,khd->qhd/dot_general | solution.py:23
  156.4 1.8 fusion.55
  158.2 0.0 reduce-scatter.2.cloned.1.call-update
  158.2 0.0 copy-start.6
  158.2 0.0 copy-start.9
  158.3 0.0 copy-start.5
  158.3 0.0 copy-start.2
  158.3 0.0 copy-start.7
  158.3 0.0 copy-start.8
  158.3 0.0 all-gather.10.cloned.1.call-start
  158.4 0.5 all-gather.10.cloned.1.call-update
  158.9 0.0 copy-done.6
  158.9 0.6 reduce-window.6
  159.5 0.2 slice_reduce_fusion
  159.8 5.2 %all-gather.2 = bf16[4,2,1024]{2,1,0:T(2,128)(2,1)S(1)} all-gather(bf16[1,2,1024]{2,1,0:T(2,128)(2,1)S(1)} %bitcast.57), channel_id=1, replica_groups=mesh['seq'=8,'type'=4] {'type'}, dimensions={0}, use_global_device_ids=true | all-gather | bytes 20480 | tf_op jit(solution)/shard_map/all_gather | solution.py:118
  165.0 6.0 %all_gather.23 = bf16[8,1024,16]{1,2,0:T(8,128)(2,1)S(1)} all-gather(bf16[2,1024,16]{1,2,0:T(8,128)(2,1)S(1)} %copy-done.5), channel_id=1, replica_groups=mesh['seq'=8,'type'=4] {'type'}, dimensions={0}, use_global_device_ids=true | all-gather | bytes 327680 | tf_op jit(solution)/shard_map/all_gather | solution.py:119
  171.0 0.1 add_bitcast_fusion
  171.1 18.1 %reduce-scatter.2.cloned.1.call-done = f32[136,1024]{1,0:T(8,128)} async-done(((f32[544,1024]{1,0:T(8,128)}), f32[136,1024]{1,0:T(8,128)}) %reduce-scatter.2.cloned.1.call-update) | async-done | bytes 557072 | tf_op jit(solution)/shard_map/reduce_scatter | solution.py:96
  189.2 0.0 copy-done.7
  189.2 1.2 fusion.32
  190.4 0.0 copy-done.8
  190.4 0.5 convolution_convert_fusion
  190.9 0.3 reshape.68
  191.2 105.4 %all-gather.10.cloned.1.call-done = bf16[8,1024,1024]{2,1,0:T(8,128)(2,1)} async-done(((bf16[2,1024,1024]{2,1,0:T(8,128)(2,1)}), bf16[8,1024,1024]{2,1,0:T(8,128)(2,1)}) %all-gather.10.cloned.1.call-update) | async-done | bytes 16777232 | tf_op jit(solution)/shard_map/all_gather | solution.py:117
  296.6 7.6 %fusion.19 = f32[8,51,16]{1,2,0:T(8,128)S(1)} fusion(bf16[8,1024,16]{1,2,0:T(8,128)(2,1)S(1)} %all_gather.23, bf16[8,51,1024]{2,1,0:T(8,128)(2,1)S(1)} %reshape.68, bf16[8,1024,1024]{2,1,0:T(8,128)(2,1)} %all-gather.10.cloned.1.call-done, f32[8,1024]{1,0:T(8,128)S(1)} %reshape.77), kind=kOutput, calls=%fused_computation.19 | convolution fusion | flops 873185280 | bytes 17933824 | tf_op jit(solution)/shard_map/...tch,tho->...tco/dot_general | solution.py:38
  304.2 0.1 reshape.69
  304.3 0.9 fusion.43
  (23 shorter events, 0.2 us)
Async XLA Ops:
  7.2 23.8 %copy-start = (bf16[3,1024,256]{2,1,0:T(8,128)(2,1)S(1)}, bf16[3,1024,256]{2,1,0:T(8,128)(2,1)}, u32[]{:S(2)}) copy-start(bf16[3,1024,256]{2,1,0:T(8,128)(2,1)} %param.14) | copy-start | bytes 4718596
  7.2 23.8 %all-gather.8.cloned.1.call-start = ((), (), s32[]{:S(2)}) async-start(), calls=%async_computation.1 | async-start | bytes 1392640 | tf_op jit(solution)/shard_map/all_gather | solution.py:50
  11.0 73.9 %all-gather.12.cloned.1.call-start = ((), (), s32[]{:S(2)}) async-start(), calls=%async_computation.4 | async-start | bytes 2506752 | tf_op jit(solution)/shard_map/all_gather | solution.py:89
  34.1 102.2 %all-gather.14.cloned.1.call-start = ((), (), s32[]{:S(2)}) async-start(), calls=%async_computation.5 | async-start | bytes 2506752 | tf_op jit(solution)/shard_map/all_gather | solution.py:90
  34.9 154.3 %reduce-scatter.2.cloned.1.call-start = ((), (), s32[]{:S(2)}) async-start(), calls=%async_computation.2 | async-start | bytes 2785280 | tf_op jit(solution)/shard_map/reduce_scatter | solution.py:96
  140.5 15.9 %copy-start.4 = (bf16[256,1024]{1,0:T(8,128)(2,1)S(1)}, bf16[256,1024]{1,0:T(8,128)(2,1)}, u32[]{:S(2)}) copy-start(bf16[256,1024]{1,0:T(8,128)(2,1)} %param.15) | copy-start | bytes 1572868
  158.2 0.7 copy-start.6
  158.2 1.5 copy-start.9
  158.3 6.7 %copy-start.5 = (bf16[2,1024,16]{1,2,0:T(8,128)(2,1)S(1)}, bf16[2,1024,16]{1,2,0:T(8,128)(2,1)}, u32[]{:S(2)}) copy-start(bf16[2,1024,16]{1,2,0:T(8,128)(2,1)} %param.19) | copy-start | bytes 196612
  158.3 30.9 %copy-start.2 = (bf16[136,1024]{1,0:T(8,128)(2,1)S(1)}, bf16[136,1024]{1,0:T(8,128)(2,1)}, u32[]{:S(2)}) copy-start(bf16[136,1024]{1,0:T(8,128)(2,1)} %param.10) | copy-start | bytes 835588
  158.3 30.9 %copy-start.7 = (f32[1024]{0:T(1024)S(1)}, f32[1024]{0:T(1024)}, u32[]{:S(2)}) copy-start(f32[1024]{0:T(1024)} %param.12) | copy-start | bytes 12292
  158.3 32.1 %copy-start.8 = (f32[1024]{0:T(1024)S(1)}, f32[1024]{0:T(1024)}, u32[]{:S(2)}) copy-start(f32[1024]{0:T(1024)} %param.13) | copy-start | bytes 12292
  158.3 138.3 %all-gather.10.cloned.1.call-start = ((), (), s32[]{:S(2)}) async-start(), calls=%async_computation.3 | async-start | bytes 20971520 | tf_op jit(solution)/shard_map/all_gather | solution.py:117
  190.4 113.8 %copy-start.3 = (bf16[136,1024]{1,0:T(8,128)(2,1)}, bf16[136,1024]{1,0:T(8,128)(2,1)S(1)}, u32[]{:S(2)}) copy-start(bf16[136,1024]{1,0:T(8,128)(2,1)S(1)} %get-tuple-element.3) | copy-start | bytes 835588
  296.6 8.6 %copy-start.1 = (bf16[3,1024,256]{2,1,0:T(8,128)(2,1)S(1)}, bf16[3,1024,256]{2,1,0:T(8,128)(2,1)}, u32[]{:S(2)}) copy-start(bf16[3,1024,256]{2,1,0:T(8,128)(2,1)} %param.14) | copy-start | bytes 4718596
Sparse Core Ops, SparseCore 0:
  11.1 19.7 all-gather.7
  34.2 50.6 all-gather.11
  87.1 49.1 all-gather.13
  158.4 30.7 reduce-scatter.1
  190.6 105.9 all-gather.9
where the time goes:
time: 312 us
  waiting for transfers between devices  209 us (67%)
  matrix products  45.1 us (14%)
  other arithmetic  22.6 us (7%)
  between operations  13.9 us (4%)
  blocking collectives  11.2 us (4%)
  local copies, waits for them, and re-layouts  9.97 us (3%)
    all_gather x1, waiting for transfers between devices, body(): lax.all_gather(head_w1, 'type', axis=0, tiled=True)  105 us
    all_gather x1, waiting for transfers between devices, body(): lax.all_gather(local_keys, 'seq', axis=0, tiled=True)  50 us
    all_gather x1, waiting for transfers between devices, body(): lax.all_gather(modulated, 'type', axis=0, tiled=True)  19.9 us
    reduce_scatter x1, waiting for transfers between devices, body(): lax.psum_scatter(jnp.dot(attended, w_out, preferred_element_type=jnp.floa...  18.1 us
    reduce_sum x1, other arithmetic, absorb_block(): totals = totals * decay + jnp.sum(weights, axis=-1)  16.8 us
    dot_general x1, matrix products, absorb_block(): jnp.einsum('qhd,khd->hqk', query_heads, key_heads, preferred_element_type...  16.1 us
    dot_general x1, matrix products, absorb_block(): jnp.einsum('hqk,khd->qhd', weights.astype(jnp.bfloat16), value_heads, pre...  15.9 us
    all_gather x1, waiting for transfers between devices, body(): lax.all_gather(local_values, 'seq', axis=0, tiled=True)  14.3 us
  transfers between devices with their start and end apart: 5, of which 5 were waited for; matrix products, arithmetic and copies ran while one was open for 13% of the time, Pallas kernels for 0%

commit v1 on v0

v1 whole, which is shorter than its diff:
```python
import functools

import jax
import jax.numpy as jnp
from jax import lax
from jax.experimental import pallas as pl
from jax.experimental.pallas import tpu as pltpu
from jax.sharding import PartitionSpec as P

HD = 64
MESH = pl.DeviceIdType.MESH
F32 = jnp.float32
BF16 = jnp.bfloat16


def rms_normalize(values):
    squares = jnp.mean(values * values, axis=-1, keepdims=True)
    return values * lax.rsqrt(squares + 1e-06)


def greet(peers):
    barrier = pltpu.get_barrier_semaphore()
    for peer in peers:
        pl.semaphore_signal(barrier, inc=1, device_id=peer, device_id_type=MESH)
    pl.semaphore_wait(barrier, len(peers))


def remote(src, dst, send, recv, peer):
    return pltpu.make_async_remote_copy(
        src_ref=src, dst_ref=dst, send_sem=send, recv_sem=recv, device_id=peer, device_id_type=MESH
    )


def partners(t):
    core = t + 1 - 2 * (t % 2)
    across = (t + 2) % 4
    diag = core + 2 - 4 * (core // 2)
    return core, across, diag


def project_kernel(
    S, HL, tok, ss, wqkv, wout, q_out, kv_out, wf_out,
    mod, proj, qsend, kvsend, m_s, m_r, w_s, w_r, q_s, q_r, k_s, k_r, f_s, f_r, l_s,
):
    G = S // HL
    s = lax.axis_index("seq")
    t = lax.axis_index("type")
    h0, g = s // G, s % G
    core, across, diag = partners(t)
    zs = [((h0 + d) % HL) * G + g for d in range(HL)]
    froms = [((h0 + HL - d) % HL) * G + g for d in range(HL)]
    groups = [h0 * G + (g + e) % G for e in range(G)]
    greet(
        [(s, core), (s, across)]
        + [(zs[d], t) for d in range(1, HL)]
        + [(groups[e], t) for e in range(1, G)]
    )
    x = tok[...].astype(F32)
    mod[t] = (rms_normalize(x) * (1.0 + ss[1:2]) + ss[0:1]).astype(BF16)
    to_across = remote(mod.at[t], mod.at[t], m_s.at[1], m_r.at[1], (s, across))
    to_across.start()
    to_core = remote(mod.at[t], mod.at[t], m_s.at[0], m_r.at[0], (s, core))
    to_core.start()

    def project(i):
        block = mod[i]
        for which in range(3):
            proj[i, :, which * 256 : which * 256 + 256] = jnp.dot(
                block, wqkv[which], preferred_element_type=F32
            )

    own_w = pltpu.make_async_copy(wout, wf_out.at[t], l_s.at[0])
    own_w.start()
    project(t)
    remote(mod.at[core], mod.at[core], m_s.at[0], m_r.at[0], (s, core)).wait_recv()
    project(core)
    remote(mod.at[across], mod.at[across], m_s.at[1], m_r.at[1], (s, across)).wait_recv()
    passed = remote(mod.at[across], mod.at[across], m_s.at[2], m_r.at[2], (s, core))
    passed.start()
    w_across = remote(wout, wf_out.at[t], w_s.at[1], w_r.at[1], (s, across))
    w_across.start()
    project(across)
    remote(mod.at[diag], mod.at[diag], m_s.at[2], m_r.at[2], (s, core)).wait_recv()
    project(diag)

    rows = proj.shape[0] * proj.shape[1]
    half = rows // 2
    for h in range(HL):
        k = proj[:, :, 256 + h * HD : 256 + h * HD + HD].reshape(rows, HD)
        v = proj[:, :, 512 + h * HD : 512 + h * HD + HD].reshape(rows, HD)
        kvsend[h] = jnp.concatenate([k, v], axis=-1).astype(BF16)
    sends = []
    for d in range(1, HL):
        hp = (h0 + d) % HL
        c = remote(kvsend.at[hp], kv_out.at[s], k_s.at[d], k_r.at[d], (zs[d], t))
        c.start()
        sends.append(c)
    own_kv = pltpu.make_async_copy(kvsend.at[h0], kv_out.at[s], l_s.at[1])
    own_kv.start()
    for e in range(1, G):
        c = remote(kvsend.at[h0], kv_out.at[s], f_s.at[0, e], f_r.at[0, e], (groups[e], t))
        c.start()
        sends.append(c)
    for h in range(HL):
        q = proj[:, :, h * HD : h * HD + HD].reshape(rows, HD)
        qsend[h] = jnp.concatenate([q[:half], q[half:]], axis=-1).astype(BF16)
    for d in range(1, HL):
        hp = (h0 + d) % HL
        c = remote(qsend.at[hp], q_out.at[h0], q_s.at[d], q_r.at[d], (zs[d], t))
        c.start()
        sends.append(c)
    own_q = pltpu.make_async_copy(qsend.at[h0], q_out.at[h0], l_s.at[2])
    own_q.start()
    w_core = remote(wout, wf_out.at[t], w_s.at[0], w_r.at[0], (s, core))
    w_core.start()

    for d in range(1, HL):
        slot = kv_out.at[froms[d]]
        remote(slot, slot, k_s.at[d], k_r.at[d], (zs[d], t)).wait_recv()
        for e in range(1, G):
            c = remote(slot, slot, f_s.at[d, e], f_r.at[d, e], (groups[e], t))
            c.start()
            sends.append(c)
    slot = wf_out.at[across]
    remote(slot, slot, w_s.at[1], w_r.at[1], (s, across)).wait_recv()
    w_passed = remote(slot, slot, w_s.at[2], w_r.at[2], (s, core))
    w_passed.start()

    for d in range(1, HL):
        slot = q_out.at[(h0 + HL - d) % HL]
        remote(slot, slot, q_s.at[d], q_r.at[d], (zs[d], t)).wait_recv()
    for d in range(HL):
        for e in range(1, G):
            slot = kv_out.at[((h0 + HL - d) % HL) * G + (g + G - e) % G]
            remote(slot, slot, f_s.at[d, e], f_r.at[d, e], (groups[e], t)).wait_recv()
    slot = wf_out.at[core]
    remote(slot, slot, w_s.at[0], w_r.at[0], (s, core)).wait_recv()
    slot = wf_out.at[diag]
    remote(slot, slot, w_s.at[2], w_r.at[2], (s, core)).wait_recv()
    for c in [to_across, to_core, passed, w_across, w_core, w_passed] + sends:
        c.wait_send()
    own_w.wait()
    own_kv.wait()
    own_q.wait()


def attend_kernel(chunk, q_ref, kv_ref, out_ref, vv, numer, top):
    keys = kv_ref.shape[0]

    @pl.when(pl.program_id(0) == 0)
    def _():
        kv = kv_ref[...]
        lane = lax.broadcasted_iota(jnp.int32, kv.shape, 1)
        vv[...] = jnp.where(lane < HD, jnp.ones_like(kv), kv)

    packed = q_ref[...]
    rows = packed.shape[0]
    zeros = jnp.zeros((rows, HD), BF16)
    factor = HD ** (-0.5)
    for half in range(2):
        q = jnp.concatenate([packed[:, half * HD : half * HD + HD], zeros], axis=-1)

        def scores_of(lo):
            return lax.dot_general(
                q, kv_ref[pl.ds(lo, chunk), :], (((1,), (1,)), ((), ())), preferred_element_type=F32
            )

        if keys == chunk:
            sc = scores_of(0)
            m = jnp.max(sc, axis=-1, keepdims=True)
            p = jnp.exp((sc - m) * factor).astype(BF16)
            o = jnp.dot(p, vv[...], preferred_element_type=F32)
        else:
            numer[...] = jnp.zeros_like(numer)
            top[...] = jnp.full_like(top, -1e30)

            def step(i, carry):
                lo = pl.multiple_of(i * chunk, chunk)
                sc = scores_of(lo)
                old = top[...]
                m = jnp.maximum(old, jnp.max(sc, axis=-1, keepdims=True))
                p = jnp.exp((sc - m) * factor).astype(BF16)
                numer[...] = numer[...] * jnp.exp((old - m) * factor) + jnp.dot(
                    p, vv[pl.ds(lo, chunk), :], preferred_element_type=F32
                )
                top[...] = m
                return carry

            lax.fori_loop(0, keys // chunk, step, 0)
            o = numer[...]
        a = o[:, HD:] / o[:, :HD]
        block = rows // 2
        for j in range(2):
            b = a[j * block : (j + 1) * block]
            out_ref[half * 2 + j] = jnp.concatenate(
                [b[0:80], b[block - 80 : block]], axis=-1
            ).astype(BF16)


def finish_kernel(
    S, HL, T, att_send, wf, tok, gate, gain, kinds, w1, b1, w2,
    upd_out, head_out,
    arecv, att, fin, rsend, rrecv, a_s, a_r, m_s, m_r, r_s, r_r, l_s,
):
    G = S // HL
    s = lax.axis_index("seq")
    t = lax.axis_index("type")
    h0, g = s // G, s % G
    core, across, diag = partners(t)
    P0 = h0 * T + t
    N = HL * T

    def device(p):
        return ((p // T) * G + g, p % T)

    peers = [(P0 + d) % N for d in range(N)]
    froms = [(P0 + N - d) % N for d in range(N)]
    greet([device(peers[d]) for d in range(1, N)])
    mine = t * HL + h0
    sends = []
    for d in range(1, N):
        c = remote(att_send.at[peers[d]], arecv.at[mine], a_s.at[d], a_r.at[d], device(peers[d]))
        c.start()
        sends.append(c)
    own = pltpu.make_async_copy(att_send.at[P0], arecv.at[mine], l_s.at[0])
    own.start()
    own.wait()
    for d in range(1, N):
        slot = arecv.at[(froms[d] % T) * HL + froms[d] // T]
        remote(slot, slot, a_s.at[d], a_r.at[d], device(peers[d])).wait_recv()
    block = tok.shape[0]
    for j in range(N // 2):
        pair = []
        for i in (2 * j, 2 * j + 1):
            r = arecv[i].astype(F32)
            pair.append(jnp.concatenate([r[:, :HD], r[160 - block : 80, HD:]], axis=0))
        att[:, 128 * j : 128 * j + 128] = jnp.concatenate(pair, axis=-1).astype(BF16)
    mixed = jnp.dot(att[...], wf[...], preferred_element_type=F32)
    updated = (tok[...].astype(F32) + gate[...] * mixed).astype(BF16)
    upd_out[...] = updated
    fin[t] = (rms_normalize(updated.astype(F32)) * gain[...]).astype(BF16)
    to_across = remote(fin.at[t], fin.at[t], m_s.at[1], m_r.at[1], (s, across))
    to_across.start()
    to_core = remote(fin.at[t], fin.at[t], m_s.at[0], m_r.at[0], (s, core))
    to_core.start()

    def heads(i, dst):
        f = fin[i]
        for k in range(2):
            hid = jnp.dot(f, w1[k], preferred_element_type=F32) + b1[k : k + 1].astype(F32)
            hid = jax.nn.gelu(hid).astype(BF16)
            dst[k * 16 : k * 16 + 16, :] = lax.dot_general(
                w2[k], hid, (((1,), (1,)), ((), ())), preferred_element_type=F32
            )

    heads(t, rrecv.at[t])
    remote(fin.at[core], fin.at[core], m_s.at[0], m_r.at[0], (s, core)).wait_recv()
    heads(core, rsend.at[0])
    c = remote(rsend.at[0], rrecv.at[t], r_s.at[0], r_r.at[0], (s, core))
    c.start()
    sends.append(c)
    remote(fin.at[across], fin.at[across], m_s.at[1], m_r.at[1], (s, across)).wait_recv()
    passed = remote(fin.at[across], fin.at[across], m_s.at[2], m_r.at[2], (s, core))
    passed.start()
    heads(across, rsend.at[1])
    c = remote(rsend.at[1], rrecv.at[t], r_s.at[1], r_r.at[1], (s, across))
    c.start()
    sends.append(c)
    remote(fin.at[diag], fin.at[diag], m_s.at[2], m_r.at[2], (s, core)).wait_recv()
    heads(diag, rsend.at[2])
    c = remote(rsend.at[2], rrecv.at[t], r_s.at[2], r_r.at[2], (s, diag))
    c.start()
    sends.append(c)
    for i, peer in enumerate((core, across, diag)):
        slot = rrecv.at[peer]
        remote(slot, slot, r_s.at[i], r_r.at[i], (s, peer)).wait_recv()
    kind = kinds[...]
    total = jnp.zeros((16, block), F32)
    for owner in range(T):
        for k in range(2):
            total = jnp.where(kind == 2 * owner + k, rrecv[owner, k * 16 : k * 16 + 16, :], total)
    head_out[...] = total
    for c in [to_across, to_core, passed] + sends:
        c.wait_send()


VM = pl.BlockSpec(memory_space=pltpu.VMEM)
HB = pl.BlockSpec(memory_space=pl.ANY)


def body(
    S, T,
    tokens, shift_scale, branch_gate, final_gain, w_qkv, w_out, type_ids, head_w1, head_b1, head_w2
):
    block, D = tokens.shape
    width = w_qkv.shape[2]
    HL = width // HD
    G = S // HL
    rows = block * T
    dma = pltpu.SemaphoreType.DMA
    q, kv, wf = pl.pallas_call(
        functools.partial(project_kernel, S, HL),
        out_shape=(
            jax.ShapeDtypeStruct((HL, rows // 2, 128), BF16),
            jax.ShapeDtypeStruct((S, rows, 128), BF16),
            jax.ShapeDtypeStruct((T, width, D), BF16),
        ),
        in_specs=[VM] * 4,
        out_specs=(HB, HB, HB),
        scratch_shapes=[
            pltpu.VMEM((T, block, D), BF16),
            pltpu.VMEM((T, block, 3 * width), F32),
            pltpu.VMEM((HL, rows // 2, 128), BF16),
            pltpu.VMEM((HL, rows, 128), BF16),
            dma((3,)), dma((3,)), dma((3,)), dma((3,)),
            dma((HL,)), dma((HL,)), dma((HL,)), dma((HL,)),
            dma((HL, G)), dma((HL, G)), dma((3,)),
        ],
        compiler_params=pltpu.CompilerParams(
            collective_id=0, has_side_effects=True, vmem_limit_bytes=40 * 2**20
        ),
        name="project",
    )(tokens, shift_scale, w_qkv, w_out)

    keys = S * rows
    chunk = 8 * rows
    att = pl.pallas_call(
        functools.partial(attend_kernel, chunk),
        grid=(HL,),
        out_shape=jax.ShapeDtypeStruct((HL * T, 80, 128), BF16),
        in_specs=[
            pl.BlockSpec((rows // 2, 128), lambda i: (i, 0)),
            pl.BlockSpec((keys, 128), lambda i: (0, 0)),
        ],
        out_specs=pl.BlockSpec((T, 80, 128), lambda i: (i, 0, 0)),
        scratch_shapes=[
            pltpu.VMEM((keys, 128), BF16),
            pltpu.VMEM((rows // 2, 128), F32),
            pltpu.VMEM((rows // 2, 1), F32),
        ],
        compiler_params=pltpu.CompilerParams(vmem_limit_bytes=56 * 2**20),
        name="attend",
    )(q.reshape(HL * (rows // 2), 128), kv.reshape(keys, 128))

    N = HL * T
    updated, heads = pl.pallas_call(
        functools.partial(finish_kernel, S, HL, T),
        out_shape=(
            jax.ShapeDtypeStruct((block, D), BF16),
            jax.ShapeDtypeStruct((16, block), F32),
        ),
        in_specs=[VM] * 9,
        out_specs=(VM, VM),
        scratch_shapes=[
            pltpu.VMEM((N, 80, 128), BF16),
            pltpu.VMEM((block, D), BF16),
            pltpu.VMEM((T, block, D), BF16),
            pltpu.VMEM((3, 32, block), F32),
            pltpu.VMEM((T, 32, block), F32),
            dma((N,)), dma((N,)), dma((3,)), dma((3,)), dma((3,)), dma((3,)), dma((1,)),
        ],
        compiler_params=pltpu.CompilerParams(
            collective_id=1, has_side_effects=True, vmem_limit_bytes=40 * 2**20
        ),
        name="finish",
    )(
        att, wf.reshape(T * width, D), tokens, branch_gate.reshape(1, D), final_gain.reshape(1, D),
        type_ids.reshape(1, block), head_w1, head_b1, jnp.transpose(head_w2, (0, 2, 1)),
    )
    return (updated, heads.T)


def solution(mesh):
    in_specs = (
        P(("seq", "type"), None),
        P(),
        P(),
        P(),
        P(None, None, "type"),
        P("type", None),
        P(("seq", "type"), None),
        P("type", None, None),
        P("type", None),
        P("type", None, None),
    )
    out_specs = (P(("seq", "type"), None), P(("seq", "type"), None))
    return jax.shard_map(
        functools.partial(body, mesh.shape["seq"], mesh.shape["type"]),
        mesh=mesh, in_specs=in_specs, out_specs=out_specs, check_vma=False,
    )
```

time: 312 us -> 93.9 us (0.30)
  waiting for transfers between devices: 209 us -> 0 us
  Pallas kernels: 0 us -> 82.5 us
  matrix products: 45.1 us -> 0 us
  other arithmetic: 22.6 us -> 0 us
  between operations: 13.9 us -> 0.73 us
  blocking collectives: 11.2 us -> 0 us
    all_gather x4 -> x0, waiting for transfers between devices: 190 us -> none  [the longest x1 105 us: body(): lax.all_gather(head_w1, 'type', axis=0, tiled=True)]
    pallas_call x0 -> x3, Pallas kernels: none -> 82.5 us  [the longest x1 34.6 us: body(): pl.pallas_call(functools.partial(project_kernel, S, HL), out_shape=(jax.S...]
    dot_general x7 -> x0, matrix products: 45.1 us -> none  [the longest x1 16.1 us: absorb_block(): jnp.einsum('qhd,khd->hqk', query_heads, key_heads, preferred_element_type...]
    reduce_sum x4 -> x0, other arithmetic: 19.2 us -> none  [the longest x1 16.8 us: absorb_block(): totals = totals * decay + jnp.sum(weights, axis=-1)]
    reduce_scatter x1 -> x0, waiting for transfers between devices: 18.1 us -> none  [body(): lax.psum_scatter(jnp.dot(attended, w_out, preferred_element_type=jnp.floa...]
    all_gather x2 -> x0, blocking collectives: 11.2 us -> none  [the longest x1 6 us: body(): lax.all_gather(head_w2, 'type', axis=0, tiled=True)]
    unnamed x20 -> x30, local copies, waits for them, and re-layouts: 0.08 us -> 10.3 us
    all_gather x2 -> x0, local copies, waits for them, and re-layouts: 8.24 us -> none  [the longest x1 4.12 us: body(): lax.all_gather(local_keys, 'seq', axis=0, tiled=True)]
  transfers between devices with their start and end apart: 5 -> 0, of which waited for: 5 -> 0; matrix products, arithmetic and copies ran while one was open for 13% -> 0% of each run, Pallas kernels for 0% -> 0%
where the time goes in v1:
time: 93.9 us; the launch traced here: 93.5 us
  Pallas kernels  82.5 us (88%)
  local copies, waits for them, and re-layouts  10.3 us (11%)
    pallas_call x1, Pallas kernels, body(): pl.pallas_call(functools.partial(project_kernel, S, HL), out_shape=(jax.S...  34.6 us
    pallas_call x1, Pallas kernels, body(): pl.pallas_call(functools.partial(finish_kernel, S, HL, T), out_shape=(jax...  29 us
    pallas_call x1, Pallas kernels, body(): pl.pallas_call(functools.partial(attend_kernel, chunk), grid=(HL,), out_s...  18.9 us
    unnamed x30, local copies, waits for them, and re-layouts  10.3 us

profile of v1, /device:TPU:0, one launch (start us, length us, event | category | flops | bytes accessed | tf_op | source)
XLA Modules:
  0.0 93.5 jit_solution(9741301184760493685)
XLA Ops:
  0.6 0.0 copy-start.13
  0.6 0.0 copy-start.10
  0.7 0.0 copy-start.1
  0.7 1.4 %copy-done.1 = bf16[3,1024,256]{2,1,0:T(8,128)(2,1)S(1)} copy-done((bf16[3,1024,256]{2,1,0:T(8,128)(2,1)S(1)}, bf16[3,1024,256]{2,1,0:T(8,128)(2,1)}, u32[]{:S(2)}) %copy-start.1) | copy-done | bytes 1572888
  2.1 0.0 copy-start.3
  2.1 1.0 %copy-done.3 = bf16[136,1024]{1,0:T(8,128)(2,1)S(1)} copy-done((bf16[136,1024]{1,0:T(8,128)(2,1)S(1)}, bf16[136,1024]{1,0:T(8,128)(2,1)}, u32[]{:S(2)}) %copy-start.3) | copy-done | bytes 278552
  3.0 0.0 copy-start.6
  3.0 1.0 %copy-done.6 = bf16[256,1024]{1,0:T(8,128)(2,1)S(1)} copy-done((bf16[256,1024]{1,0:T(8,128)(2,1)S(1)}, bf16[256,1024]{1,0:T(8,128)(2,1)}, u32[]{:S(2)}) %copy-start.6) | copy-done | bytes 524312
  4.1 0.0 copy-start.9
  4.1 0.7 copy-done.9
  4.8 0.0 copy-start.4
  4.8 0.0 copy-start.8
  4.8 0.0 copy-start.11
  4.8 0.0 copy-start.12
  4.8 34.6 %project.1 = (bf16[4,272,128]{2,1,0:T(8,128)(2,1)S(1)}, bf16[8,544,128]{2,1,0:T(8,128)(2,1)S(1)}, bf16[4,256,1024]{2,1,0:T(8,128)(2,1)S(1)}) custom-call(bf16[136,1024]{1,0:T(8,128)(2,1)S(1)} %copy-done.3, f32[2,1024]{1,0:T(2,128)S(1)} %copy-done.9, bf16[3,1024,256]{2,1,0:T(8,128)(2,1)S(1)} %copy-done.1, bf16[256,1024]{1,0:T(8,128)(2,1)S(1)} %copy-done.6), custom_call_target="tpu_custom_call" | custom-call | tf_op jit(solution)/shard_map/project/pallas_call | solution.py:301
  39.4 0.0 copy-start.5
  39.4 1.0 %copy-done.5 = bf16[8,544,128]{2,1,0:T(8,128)(2,1)} copy-done((bf16[8,544,128]{2,1,0:T(8,128)(2,1)}, bf16[8,544,128]{2,1,0:T(8,128)(2,1)S(1)}, u32[]{:S(2)}) %copy-start.5) | copy-done | bytes 1114136
  40.4 0.0 copy-start.7
  40.4 0.7 copy-done.7
  41.1 18.9 %attend.1.att_send = bf16[16,80,128]{2,1,0:T(8,128)(2,1)} custom-call(bf16[1088,128]{1,0:T(8,128)(2,1)} %bitcast.10, bf16[4352,128]{1,0:T(8,128)(2,1)} %bitcast.9), custom_call_target="tpu_custom_call" | custom-call | tf_op jit(solution)/shard_map/attend/pallas_call | solution.py:327
  60.0 0.0 copy-done.13
  60.0 0.0 copy-done.10
  60.0 0.0 copy-done.4
  60.1 0.0 copy-done.8
  60.1 0.0 copy-done.11
  60.1 0.0 copy-done.12
  60.1 0.0 copy-start
  60.1 2.2 %copy-done = bf16[2,1024,1024]{2,1,0:T(8,128)(2,1)S(1)} copy-done((bf16[2,1024,1024]{2,1,0:T(8,128)(2,1)S(1)}, bf16[2,1024,1024]{2,1,0:T(8,128)(2,1)}, u32[]{:S(2)}) %copy-start) | copy-done | bytes 4194328
  62.3 0.0 copy-start.2
  62.3 1.0 %copy-done.2 = bf16[16,80,128]{2,1,0:T(8,128)(2,1)S(1)} copy-done((bf16[16,80,128]{2,1,0:T(8,128)(2,1)S(1)}, bf16[16,80,128]{2,1,0:T(8,128)(2,1)}, u32[]{:S(2)}) %copy-start.2) | copy-done | bytes 327704
  63.2 29.0 %finish.1 = (bf16[136,1024]{1,0:T(8,128)(2,1)S(1)}, f32[16,136]{1,0:T(8,128)S(1)}) custom-call(bf16[16,80,128]{2,1,0:T(8,128)(2,1)S(1)} %copy-done.2, bf16[1024,1024]{1,0:T(8,128)(2,1)S(1)} %bitcast.8, bf16[136,1024]{1,0:T(8,128)(2,1)S(1)} %copy-done.4, f32[1,1024]{1,0:T(1,128)S(1)} %bitcast.13, f32[1,1024]{1,0:T(1,128)S(1)} %bitcast.14, ...), custom_call_target="tpu_custom_call" | custom-call | tf_op jit(solution)/shard_map/finish/pallas_call | solution.py:346
  92.2 0.7 copy.14
  92.9 0.6 copy.15
Async XLA Ops:
  0.6 59.4 %copy-start.13 = (s32[136,1]{0,1:T(1,128)S(1)}, s32[136,1]{0,1:T(1,128)}, u32[]{:S(2)}) copy-start(s32[136,1]{0,1:T(1,128)} %param.16) | copy-start | bytes 1636
  0.6 59.4 %copy-start.10 = (f32[1024]{0:T(1024)S(1)}, f32[1024]{0:T(1024)}, u32[]{:S(2)}) copy-start(f32[1024]{0:T(1024)} %param.12) | copy-start | bytes 12292
  0.7 1.4 %copy-start.1 = (bf16[3,1024,256]{2,1,0:T(8,128)(2,1)S(1)}, bf16[3,1024,256]{2,1,0:T(8,128)(2,1)}, u32[]{:S(2)}) copy-start(bf16[3,1024,256]{2,1,0:T(8,128)(2,1)} %wqkv.1) | copy-start | bytes 4718596
  2.1 1.0 %copy-start.3 = (bf16[136,1024]{1,0:T(8,128)(2,1)S(1)}, bf16[136,1024]{1,0:T(8,128)(2,1)}, u32[]{:S(2)}) copy-start(bf16[136,1024]{1,0:T(8,128)(2,1)} %tok.3) | copy-start | bytes 835588
  3.0 1.0 %copy-start.6 = (bf16[256,1024]{1,0:T(8,128)(2,1)S(1)}, bf16[256,1024]{1,0:T(8,128)(2,1)}, u32[]{:S(2)}) copy-start(bf16[256,1024]{1,0:T(8,128)(2,1)} %wout.1) | copy-start | bytes 1572868
  4.1 0.7 copy-start.9
  4.8 55.3 %copy-start.4 = (bf16[136,1024]{1,0:T(8,128)(2,1)S(1)}, bf16[136,1024]{1,0:T(8,128)(2,1)}, u32[]{:S(2)}) copy-start(bf16[136,1024]{1,0:T(8,128)(2,1)} %tok.3) | copy-start | bytes 835588
  4.8 55.3 %copy-start.8 = (bf16[2,1024,16]{1,2,0:T(8,128)(2,1)S(1)}, bf16[2,1024,16]{1,2,0:T(8,128)(2,1)}, u32[]{:S(2)}) copy-start(bf16[2,1024,16]{1,2,0:T(8,128)(2,1)} %param.19) | copy-start | bytes 196612
  4.8 55.3 %copy-start.11 = (f32[1024]{0:T(1024)S(1)}, f32[1024]{0:T(1024)}, u32[]{:S(2)}) copy-start(f32[1024]{0:T(1024)} %param.13) | copy-start | bytes 12292
  4.8 55.3 %copy-start.12 = (bf16[2,1024]{1,0:T(2,128)(2,1)S(1)}, bf16[2,1024]{1,0:T(2,128)(2,1)}, u32[]{:S(2)}) copy-start(bf16[2,1024]{1,0:T(2,128)(2,1)} %b1.1) | copy-start | bytes 12292
  39.4 1.0 %copy-start.5 = (bf16[8,544,128]{2,1,0:T(8,128)(2,1)}, bf16[8,544,128]{2,1,0:T(8,128)(2,1)S(1)}, u32[]{:S(2)}) copy-start(bf16[8,544,128]{2,1,0:T(8,128)(2,1)S(1)} %get-tuple-element.8) | copy-start | bytes 3342340
  40.4 0.7 copy-start.7
  60.1 2.2 %copy-start = (bf16[2,1024,1024]{2,1,0:T(8,128)(2,1)S(1)}, bf16[2,1024,1024]{2,1,0:T(8,128)(2,1)}, u32[]{:S(2)}) copy-start(bf16[2,1024,1024]{2,1,0:T(8,128)(2,1)} %w1.1) | copy-start | bytes 12582916
  62.3 1.0 %copy-start.2 = (bf16[16,80,128]{2,1,0:T(8,128)(2,1)S(1)}, bf16[16,80,128]{2,1,0:T(8,128)(2,1)}, u32[]{:S(2)}) copy-start(bf16[16,80,128]{2,1,0:T(8,128)(2,1)} %attend.1.att_send) | copy-start | bytes 983044

commit v2 on v0

v2 whole, which is shorter than its diff:
```python
import functools

import jax
import jax.numpy as jnp
from jax import lax
from jax.experimental import pallas as pl
from jax.experimental.pallas import tpu as pltpu
from jax.sharding import PartitionSpec as P

HD = 64
MESH = pl.DeviceIdType.MESH
F32 = jnp.float32
BF16 = jnp.bfloat16


def rms_normalize(values):
    squares = jnp.mean(values * values, axis=-1, keepdims=True)
    return values * lax.rsqrt(squares + 1e-06)


def greet(peers):
    barrier = pltpu.get_barrier_semaphore()
    for peer in peers:
        pl.semaphore_signal(barrier, inc=1, device_id=peer, device_id_type=MESH)
    pl.semaphore_wait(barrier, len(peers))


def remote(src, dst, send, recv, peer):
    return pltpu.make_async_remote_copy(
        src_ref=src, dst_ref=dst, send_sem=send, recv_sem=recv, device_id=peer, device_id_type=MESH
    )


def partners(t):
    core = t + 1 - 2 * (t % 2)
    across = (t + 2) % 4
    diag = core + 2 - 4 * (core // 2)
    return core, across, diag


def kernel(
    S, HL, T,
    tok, ss, wqkv, wout, gate, gain, kinds, w1, b1, w2,
    upd_out, head_out,
    wq, wf, w1v, mod, proj, qsend, kvsend, qrecv, kv, qpad, vv, numer, top,
    asend, arecv, att, fin, rsend, rrecv,
    m_s, m_r, w_s, w_r, q_s, q_r, k_s, k_r, f_s, f_r, a_s, a_r, n_s, n_r, r_s, r_r, l_s,
):
    G = S // HL
    N = HL * T
    s = lax.axis_index("seq")
    t = lax.axis_index("type")
    h0, g = s // G, s % G
    core, across, diag = partners(t)
    zs = [((h0 + d) % HL) * G + g for d in range(HL)]
    groups = [h0 * G + (g + e) % G for e in range(G)]
    back = [(h0 + HL - d) % HL for d in range(HL)]
    block = tok.shape[0]
    rows = T * block
    half = rows // 2

    load_q = pltpu.make_async_copy(wqkv, wq, l_s.at[0])
    load_q.start()
    load_o = pltpu.make_async_copy(wout, wf.at[t], l_s.at[1])
    load_o.start()
    load_1 = pltpu.make_async_copy(w1, w1v, l_s.at[2])
    load_1.start()

    def device(h, tt):
        return (h * G + g, tt)

    greet(
        [
            device((h0 + d) % HL, (t + c) % T)
            for d in range(HL) for c in range(T) if d or c
        ]
        + [(groups[e], t) for e in range(1, G)]
    )
    x = tok[...].astype(F32)
    mod[t] = (rms_normalize(x) * (1.0 + ss[1:2]) + ss[0:1]).astype(BF16)
    sends = []

    def send(src, dst, a, b, peer):
        c = remote(src, dst, a, b, peer)
        c.start()
        sends.append(c)

    def arrive(slot, a, b):
        remote(slot, slot, a, b, (s, core)).wait_recv()

    send(mod.at[t], mod.at[t], m_s.at[1], m_r.at[1], (s, across))
    send(mod.at[t], mod.at[t], m_s.at[0], m_r.at[0], (s, core))

    def project(i):
        value = mod[i]
        for which in range(3):
            proj[i, :, which * 256 : which * 256 + 256] = jnp.dot(
                value, wq[which], preferred_element_type=F32
            )

    load_q.wait()
    project(t)
    arrive(mod.at[core], m_s.at[0], m_r.at[0])
    project(core)
    arrive(mod.at[across], m_s.at[1], m_r.at[1])
    send(mod.at[across], mod.at[across], m_s.at[2], m_r.at[2], (s, core))
    send(wout, wf.at[t], w_s.at[1], w_r.at[1], (s, across))
    project(across)
    arrive(mod.at[diag], m_s.at[2], m_r.at[2])
    project(diag)

    for h in range(HL):
        q = proj[:, :, h * HD : h * HD + HD].reshape(rows, HD)
        qsend[h] = jnp.concatenate([q[:half], q[half:]], axis=-1).astype(BF16)
    for d in range(1, HL):
        hp = (h0 + d) % HL
        send(qsend.at[hp], qrecv.at[h0], q_s.at[d], q_r.at[d], (zs[d], t))
    own_q = pltpu.make_async_copy(qsend.at[h0], qrecv.at[h0], l_s.at[3])
    own_q.start()
    for h in range(HL):
        k = proj[:, :, 256 + h * HD : 256 + h * HD + HD].reshape(rows, HD)
        v = proj[:, :, 512 + h * HD : 512 + h * HD + HD].reshape(rows, HD)
        kvsend[h] = jnp.concatenate([k, v], axis=-1).astype(BF16)
    for e in range(1, G):
        send(kvsend.at[h0], kv.at[s], f_s.at[0, e], f_r.at[0, e], (groups[e], t))
    own_kv = pltpu.make_async_copy(kvsend.at[h0], kv.at[s], l_s.at[4])
    own_kv.start()
    for d in range(1, HL):
        hp = (h0 + d) % HL
        send(kvsend.at[hp], kv.at[s], k_s.at[d], k_r.at[d], (zs[d], t))
    send(wout, wf.at[t], w_s.at[0], w_r.at[0], (s, core))

    def unpack(h):
        value = qrecv[h]
        zeros = jnp.zeros((half, HD), BF16)
        qpad[h * 2] = jnp.concatenate([value[:, :HD], zeros], axis=-1)
        qpad[h * 2 + 1] = jnp.concatenate([value[:, HD:], zeros], axis=-1)

    own_q.wait()
    unpack(h0)
    for d in range(1, HL):
        arrive(qrecv.at[back[d]], q_s.at[d], q_r.at[d])
        unpack(back[d])
    own_kv.wait()

    factor = HD ** (-0.5) * 1.4426950408889634
    chunks = max(G // 2, 1)
    per = G // chunks

    def keys_of(d, j):
        return kv[pl.ds(back[d] * G + j * per, per)].reshape(per * rows, 128)

    def values(d, j):
        value = keys_of(d, j)
        lane = lax.broadcasted_iota(jnp.int32, value.shape, 1)
        vv[...] = jnp.where(lane < HD, jnp.ones_like(value), value)

    def pair(d, j, h, first):
        kc = keys_of(d, j)
        scores = [
            lax.dot_general(
                qpad[h * 2 + i], kc, (((1,), (1,)), ((), ())), preferred_element_type=F32
            )
            for i in range(2)
        ]
        for i in range(2):
            sc = scores[i]
            m = jnp.max(sc, axis=-1, keepdims=True)
            if not first:
                old = top[h * 2 + i]
                m = jnp.maximum(m, old)
            p = jnp.exp2((sc - m) * factor).astype(BF16)
            o = jnp.dot(p, vv[...], preferred_element_type=F32)
            if not first:
                o = o + numer[h * 2 + i] * jnp.exp2((old - m) * factor)
            numer[h * 2 + i] = o
            top[h * 2 + i] = m

    def absorb(d, first_h, count):
        first = d == 0 and chunks == 1

        def over_chunks(j, carry):
            values(d, j)

            def over(i, inner):
                pair(d, j, (first_h + i) % HL, first)
                return inner

            lax.fori_loop(0, count, over, 0)
            return carry

        if chunks == 1:
            over_chunks(0, 0)
        else:
            lax.fori_loop(0, chunks, over_chunks, 0)

    if chunks > 1:
        numer[...] = jnp.zeros_like(numer)
        top[...] = jnp.full_like(top, -1e30)

    def group_arrives(d):
        for e in range(1, G):
            arrive(kv.at[back[d] * G + (g + G - e) % G], f_s.at[d, e], f_r.at[d, e])

    def emit(h):
        parts = []
        for i in range(2):
            o = numer[h * 2 + i]
            a = o[:, HD:] / o[:, :HD]
            for j in range(2):
                b = a[j * block : (j + 1) * block]
                asend[h * T + i * 2 + j] = jnp.concatenate(
                    [b[0:80], b[block - 80 : block]], axis=-1
                ).astype(BF16)

    mine = t * HL + h0
    group_arrives(0)
    for d in range(HL - 1):
        absorb(d, h0, HL // 2)
        slot = kv.at[back[d + 1] * G + g]
        arrive(slot, k_s.at[d + 1], k_r.at[d + 1])
        for e in range(1, G):
            send(slot, slot, f_s.at[d + 1, e], f_r.at[d + 1, e], (groups[e], t))
        if d == 0:
            arrive(wf.at[across], w_s.at[1], w_r.at[1])
            send(wf.at[across], wf.at[across], w_s.at[2], w_r.at[2], (s, core))
        absorb(d, h0 + HL // 2, HL // 2)
        group_arrives(d + 1)
    for i in range(HL):
        d = (i + 1) % HL
        h = (h0 + d) % HL
        absorb(HL - 1, h, 1)
        emit(h)
        for c in range(T):
            if d or c:
                tt = (t + c) % T
                send(
                    asend.at[h * T + tt], arecv.at[mine], a_s.at[d, c], a_r.at[d, c],
                    device(h, tt),
                )
    own_a = pltpu.make_async_copy(asend.at[h0 * T + t], arecv.at[mine], l_s.at[5])
    own_a.start()
    arrive(wf.at[core], w_s.at[0], w_r.at[0])
    arrive(wf.at[diag], w_s.at[2], w_r.at[2])
    load_o.wait()
    own_a.wait()
    for i in range(HL):
        d = (i + 1) % HL
        for c in range(T):
            if d or c:
                arrive(arecv.at[((t + T - c) % T) * HL + back[d]], a_s.at[d, c], a_r.at[d, c])
    for j in range(N // 2):
        both = []
        for i in (2 * j, 2 * j + 1):
            r = arecv[i].astype(F32)
            both.append(jnp.concatenate([r[:, :HD], r[160 - block : 80, HD:]], axis=0))
        att[:, 128 * j : 128 * j + 128] = jnp.concatenate(both, axis=-1).astype(BF16)
    mixed = jnp.dot(
        att[...], wf[...].reshape(N * HD, tok.shape[1]), preferred_element_type=F32
    )
    updated = (tok[...].astype(F32) + gate[...] * mixed).astype(BF16)
    upd_out[...] = updated
    fin[t] = (rms_normalize(updated.astype(F32)) * gain[...]).astype(BF16)
    send(fin.at[t], fin.at[t], n_s.at[1], n_r.at[1], (s, across))
    send(fin.at[t], fin.at[t], n_s.at[0], n_r.at[0], (s, core))

    def heads(i, dst):
        f = fin[i]
        for k in range(2):
            hid = jnp.dot(f, w1v[k], preferred_element_type=F32) + b1[k : k + 1].astype(F32)
            hid = jax.nn.gelu(hid).astype(BF16)
            dst[k * 16 : k * 16 + 16, :] = lax.dot_general(
                w2[k], hid, (((1,), (1,)), ((), ())), preferred_element_type=F32
            )

    load_1.wait()
    heads(t, rrecv.at[t])
    arrive(fin.at[core], n_s.at[0], n_r.at[0])
    heads(core, rsend.at[0])
    send(rsend.at[0], rrecv.at[t], r_s.at[0], r_r.at[0], (s, core))
    arrive(fin.at[across], n_s.at[1], n_r.at[1])
    send(fin.at[across], fin.at[across], n_s.at[2], n_r.at[2], (s, core))
    heads(across, rsend.at[1])
    send(rsend.at[1], rrecv.at[t], r_s.at[1], r_r.at[1], (s, across))
    arrive(fin.at[diag], n_s.at[2], n_r.at[2])
    heads(diag, rsend.at[2])
    send(rsend.at[2], rrecv.at[t], r_s.at[2], r_r.at[2], (s, diag))
    for i, peer in enumerate((core, across, diag)):
        arrive(rrecv.at[peer], r_s.at[i], r_r.at[i])
    kind = kinds[...]
    total = jnp.zeros((16, block), F32)
    for owner in range(T):
        for k in range(2):
            total = jnp.where(kind == 2 * owner + k, rrecv[owner, k * 16 : k * 16 + 16, :], total)
    head_out[...] = total
    for c in sends:
        c.wait_send()


VM = pl.BlockSpec(memory_space=pltpu.VMEM)
HB = pl.BlockSpec(memory_space=pltpu.HBM)


def body(
    S, T,
    tokens, shift_scale, branch_gate, final_gain, w_qkv, w_out, type_ids, head_w1, head_b1, head_w2
):
    block, D = tokens.shape
    width = w_qkv.shape[2]
    HL = width // HD
    G = S // HL
    N = HL * T
    rows = block * T
    half = rows // 2
    per = min(G, 2)
    dma = pltpu.SemaphoreType.DMA
    updated, heads = pl.pallas_call(
        functools.partial(kernel, S, HL, T),
        out_shape=(
            jax.ShapeDtypeStruct((block, D), BF16),
            jax.ShapeDtypeStruct((16, block), F32),
        ),
        in_specs=[VM, VM, HB, HB, VM, VM, VM, HB, VM, VM],
        out_specs=(VM, VM),
        scratch_shapes=[
            pltpu.VMEM(w_qkv.shape, BF16),
            pltpu.VMEM((T, width, D), BF16),
            pltpu.VMEM(head_w1.shape, BF16),
            pltpu.VMEM((T, block, D), BF16),
            pltpu.VMEM((T, block, 3 * width), F32),
            pltpu.VMEM((HL, half, 128), BF16),
            pltpu.VMEM((HL, rows, 128), BF16),
            pltpu.VMEM((HL, half, 128), BF16),
            pltpu.VMEM((S, rows, 128), BF16),
            pltpu.VMEM((2 * HL, half, 128), BF16),
            pltpu.VMEM((per * rows, 128), BF16),
            pltpu.VMEM((2 * HL, half, 128), F32),
            pltpu.VMEM((2 * HL, half, 1), F32),
            pltpu.VMEM((N, 80, 128), BF16),
            pltpu.VMEM((N, 80, 128), BF16),
            pltpu.VMEM((block, D), BF16),
            pltpu.VMEM((T, block, D), BF16),
            pltpu.VMEM((3, 32, block), F32),
            pltpu.VMEM((T, 32, block), F32),
            dma((3,)), dma((3,)), dma((3,)), dma((3,)),
            dma((HL,)), dma((HL,)), dma((HL,)), dma((HL,)),
            dma((HL, G)), dma((HL, G)), dma((HL, T)), dma((HL, T)),
            dma((3,)), dma((3,)), dma((3,)), dma((3,)), dma((6,)),
        ],
        compiler_params=pltpu.CompilerParams(
            collective_id=0, has_side_effects=True, vmem_limit_bytes=48 * 2**20
        ),
        name="sublayer",
    )(
        tokens, shift_scale, w_qkv, w_out, branch_gate.reshape(1, D), final_gain.reshape(1, D),
        type_ids.reshape(1, block), head_w1, head_b1, jnp.transpose(head_w2, (0, 2, 1)),
    )
    return (updated, heads.T)


def solution(mesh):
    in_specs = (
        P(("seq", "type"), None),
        P(),
        P(),
        P(),
        P(None, None, "type"),
        P("type", None),
        P(("seq", "type"), None),
        P("type", None, None),
        P("type", None),
        P("type", None, None),
    )
    out_specs = (P(("seq", "type"), None), P(("seq", "type"), None))
    return jax.shard_map(
        functools.partial(body, mesh.shape["seq"], mesh.shape["type"]),
        mesh=mesh, in_specs=in_specs, out_specs=out_specs, check_vma=False,
    )
```

time: 312 us -> 84.7 us (0.27)
  waiting for transfers between devices: 209 us -> 0 us
  Pallas kernels: 0 us -> 74.6 us
  matrix products: 45.1 us -> 0 us
  other arithmetic: 22.6 us -> 0 us
  between operations: 13.9 us -> 0.66 us
  blocking collectives: 11.2 us -> 0 us
    all_gather x4 -> x0, waiting for transfers between devices: 190 us -> none  [the longest x1 105 us: body(): lax.all_gather(head_w1, 'type', axis=0, tiled=True)]
    pallas_call x0 -> x1, Pallas kernels: none -> 74.6 us  [body(): pl.pallas_call(functools.partial(kernel, S, HL, T), out_shape=(jax.ShapeD...]
    dot_general x7 -> x0, matrix products: 45.1 us -> none  [the longest x1 16.1 us: absorb_block(): jnp.einsum('qhd,khd->hqk', query_heads, key_heads, preferred_element_type...]
    reduce_sum x4 -> x0, other arithmetic: 19.2 us -> none  [the longest x1 16.8 us: absorb_block(): totals = totals * decay + jnp.sum(weights, axis=-1)]
    reduce_scatter x1 -> x0, waiting for transfers between devices: 18.1 us -> none  [body(): lax.psum_scatter(jnp.dot(attended, w_out, preferred_element_type=jnp.floa...]
    all_gather x2 -> x0, blocking collectives: 11.2 us -> none  [the longest x1 6 us: body(): lax.all_gather(head_w2, 'type', axis=0, tiled=True)]
    unnamed x20, local copies, waits for them, and re-layouts: 0.08 us -> 8.99 us
    all_gather x2 -> x0, local copies, waits for them, and re-layouts: 8.24 us -> none  [the longest x1 4.12 us: body(): lax.all_gather(local_keys, 'seq', axis=0, tiled=True)]
  transfers between devices with their start and end apart: 5 -> 0, of which waited for: 5 -> 0; matrix products, arithmetic and copies ran while one was open for 13% -> 0% of each run, Pallas kernels for 0% -> 0%
where the time goes in v2:
time: 84.7 us; the launch traced here: 84.2 us
  Pallas kernels  74.6 us (88%)
  local copies, waits for them, and re-layouts  8.99 us (11%)
    pallas_call x1, Pallas kernels, body(): pl.pallas_call(functools.partial(kernel, S, HL, T), out_shape=(jax.ShapeD...  74.6 us
    unnamed x20, local copies, waits for them, and re-layouts  8.99 us

profile of v2, /device:TPU:0, one launch (start us, length us, event | category | flops | bytes accessed | tf_op | source)
XLA Modules:
  0.0 84.2 jit_solution(9706826860407526374)
XLA Ops:
  0.6 0.0 copy-start
  0.6 1.4 %copy-done = bf16[3,1024,256]{2,1,0:T(8,128)(2,1)S(1)} copy-done((bf16[3,1024,256]{2,1,0:T(8,128)(2,1)S(1)}, bf16[3,1024,256]{2,1,0:T(8,128)(2,1)}, u32[]{:S(2)}) %copy-start) | copy-done | bytes 1572888
  2.0 0.0 copy-start.1
  2.0 1.0 %copy-done.1 = bf16[256,1024]{1,0:T(8,128)(2,1)S(1)} copy-done((bf16[256,1024]{1,0:T(8,128)(2,1)S(1)}, bf16[256,1024]{1,0:T(8,128)(2,1)}, u32[]{:S(2)}) %copy-start.1) | copy-done | bytes 524312
  3.1 0.0 copy-start.2
  3.1 1.0 %copy-done.2 = bf16[136,1024]{1,0:T(8,128)(2,1)S(1)} copy-done((bf16[136,1024]{1,0:T(8,128)(2,1)S(1)}, bf16[136,1024]{1,0:T(8,128)(2,1)}, u32[]{:S(2)}) %copy-start.2) | copy-done | bytes 278552
  4.0 0.0 copy-start.3
  4.0 0.8 copy-done.3
  4.9 0.0 copy-start.4
  4.9 0.7 copy-done.4
  5.6 0.0 copy-start.5
  5.6 0.7 copy-done.5
  6.3 0.0 copy-start.6
  6.3 0.7 copy-done.6
  7.0 0.0 copy-start.7
  7.0 0.7 copy-done.7
  7.6 0.0 copy-start.8
  7.6 0.7 copy-done.8
  8.3 74.6 %sublayer.1 = (bf16[136,1024]{1,0:T(8,128)(2,1)S(1)}, f32[16,136]{1,0:T(8,128)S(1)}) custom-call(bf16[136,1024]{1,0:T(8,128)(2,1)S(1)} %copy-done.2, f32[2,1024]{1,0:T(2,128)S(1)} %copy-done.4, bf16[3,1024,256]{2,1,0:T(8,128)(2,1)S(1)} %copy-done, bf16[256,1024]{1,0:T(8,128)(2,1)S(1)} %copy-done.1, f32[1,1024]{1,0:T(1,128)S(1)} %bitcast.7, ...), custom_call_target="tpu_custom_call" | custom-call | tf_op jit(solution)/shard_map/sublayer/pallas_call | solution.py:317
  82.9 0.7 copy.14
  83.6 0.6 copy.15
Async XLA Ops:
  0.6 1.4 %copy-start = (bf16[3,1024,256]{2,1,0:T(8,128)(2,1)S(1)}, bf16[3,1024,256]{2,1,0:T(8,128)(2,1)}, u32[]{:S(2)}) copy-start(bf16[3,1024,256]{2,1,0:T(8,128)(2,1)} %wqkv.1) | copy-start | bytes 4718596
  2.0 1.0 %copy-start.1 = (bf16[256,1024]{1,0:T(8,128)(2,1)S(1)}, bf16[256,1024]{1,0:T(8,128)(2,1)}, u32[]{:S(2)}) copy-start(bf16[256,1024]{1,0:T(8,128)(2,1)} %wout.1) | copy-start | bytes 1572868
  3.1 1.0 %copy-start.2 = (bf16[136,1024]{1,0:T(8,128)(2,1)S(1)}, bf16[136,1024]{1,0:T(8,128)(2,1)}, u32[]{:S(2)}) copy-start(bf16[136,1024]{1,0:T(8,128)(2,1)} %tok.1) | copy-start | bytes 835588
  4.0 0.8 copy-start.3
  4.9 0.7 copy-start.4
  5.6 0.7 copy-start.5
  6.3 0.7 copy-start.6
  7.0 0.7 copy-start.7
  7.6 0.7 copy-start.8

commit v3 on v2

--- a/solution.py
+++ b/solution.py
@@ -40,8 +40,9 @@
 
 def kernel(
     S, HL, T,
-    tok, ss, wqkv, wout, gate, gain, kinds, w1, b1, w2,
+    tok_h, ss_h, wqkv, wout, gate_h, gain_h, kinds_h, w1, b1_h, w2_h,
     upd_out, head_out,
+    tok, ss, gate, gain, kinds, b1, w2, i_s,
     wq, wf, w1v, mod, proj, qsend, kvsend, qrecv, kv, qpad, vv, numer, top,
     asend, arecv, att, fin, rsend, rrecv,
     m_s, m_r, w_s, w_r, q_s, q_r, k_s, k_r, f_s, f_r, a_s, a_r, n_s, n_r, r_s, r_r, l_s,
@@ -55,10 +56,21 @@
     zs = [((h0 + d) % HL) * G + g for d in range(HL)]
     groups = [h0 * G + (g + e) % G for e in range(G)]
     back = [(h0 + HL - d) % HL for d in range(HL)]
-    block = tok.shape[0]
+    block = tok_h.shape[0]
     rows = T * block
     half = rows // 2
 
+    loads = [
+        pltpu.make_async_copy(a, b, i_s.at[i])
+        for i, (a, b) in enumerate(
+            (
+                (tok_h, tok), (ss_h, ss), (gate_h, gate), (gain_h, gain), (kinds_h, kinds),
+                (b1_h, b1), (w2_h, w2),
+            )
+        )
+    ]
+    for c in loads:
+        c.start()
     load_q = pltpu.make_async_copy(wqkv, wq, l_s.at[0])
     load_q.start()
     load_o = pltpu.make_async_copy(wout, wf.at[t], l_s.at[1])
@@ -76,10 +88,20 @@
         ]
         + [(groups[e], t) for e in range(1, G)]
     )
+    sends = []
+    mid = tok.shape[1] // 2
+
+    def keep(ref, value):
+        ref[t, 0] = value[:, :mid]
+        ref[t, 1] = value[:, mid:]
+
+    def whole(ref, i):
+        return jnp.concatenate([ref[i, 0], ref[i, 1]], axis=-1)
+
+    for c in loads:
+        c.wait()
     x = tok[...].astype(F32)
-    mod[t] = (rms_normalize(x) * (1.0 + ss[1:2]) + ss[0:1]).astype(BF16)
-    sends = []
-
+    keep(mod, (rms_normalize(x) * (1.0 + ss[1:2]) + ss[0:1]).astype(BF16))
     def send(src, dst, a, b, peer):
         c = remote(src, dst, a, b, peer)
         c.start()
@@ -88,50 +110,66 @@
     def arrive(slot, a, b):
         remote(slot, slot, a, b, (s, core)).wait_recv()
 
-    send(mod.at[t], mod.at[t], m_s.at[1], m_r.at[1], (s, across))
-    send(mod.at[t], mod.at[t], m_s.at[0], m_r.at[0], (s, core))
+    for c in range(2):
+        send(mod.at[t, c], mod.at[t, c], m_s.at[1, c], m_r.at[1, c], (s, across))
+    for c in range(2):
+        send(mod.at[t, c], mod.at[t, c], m_s.at[0, c], m_r.at[0, c], (s, core))
 
     def project(i):
-        value = mod[i]
+        value = whole(mod, i)
         for which in range(3):
             proj[i, :, which * 256 : which * 256 + 256] = jnp.dot(
                 value, wq[which], preferred_element_type=F32
             )
 
+    def ship(p):
+        y = (t // 2 + p) % 2
+        for h in range(HL):
+            lo = proj[2 * y, :, h * HD : h * HD + HD]
+            hi = proj[2 * y + 1, :, h * HD : h * HD + HD]
+            qsend[h, y] = jnp.concatenate([lo, hi], axis=-1).astype(BF16)
+            k = proj[pl.ds(2 * y, 2), :, 256 + h * HD : 256 + h * HD + HD].reshape(half, HD)
+            v = proj[pl.ds(2 * y, 2), :, 512 + h * HD : 512 + h * HD + HD].reshape(half, HD)
+            kvsend[h, y] = jnp.concatenate([k, v], axis=-1).astype(BF16)
+        for e in range(1, G):
+            send(kvsend.at[h0, y], kv.at[s, y], f_s.at[0, e, p], f_r.at[0, e, p], (groups[e], t))
+        for d in range(1, HL):
+            hp = (h0 + d) % HL
+            send(qsend.at[hp, y], qrecv.at[h0, y], q_s.at[d, p], q_r.at[d, p], (zs[d], t))
+            send(kvsend.at[hp, y], kv.at[s, y], k_s.at[d, p], k_r.at[d, p], (zs[d], t))
+
+    def pass_on(d, p):
+        y = (t // 2 + p) % 2
+        slot = kv.at[back[d] * G + g, y]
+        arrive(slot, k_s.at[d, p], k_r.at[d, p])
+        for e in range(1, G):
+            send(slot, slot, f_s.at[d, e, p], f_r.at[d, e, p], (groups[e], t))
+
     load_q.wait()
     project(t)
-    arrive(mod.at[core], m_s.at[0], m_r.at[0])
+    for c in range(2):
+        arrive(mod.at[core, c], m_s.at[0, c], m_r.at[0, c])
     project(core)
-    arrive(mod.at[across], m_s.at[1], m_r.at[1])
-    send(mod.at[across], mod.at[across], m_s.at[2], m_r.at[2], (s, core))
+    ship(0)
+    for c in range(2):
+        slot = mod.at[across, c]
+        arrive(slot, m_s.at[1, c], m_r.at[1, c])
+        send(slot, slot, m_s.at[2, c], m_r.at[2, c], (s, core))
     send(wout, wf.at[t], w_s.at[1], w_r.at[1], (s, across))
     project(across)
-    arrive(mod.at[diag], m_s.at[2], m_r.at[2])
+    for c in range(2):
+        arrive(mod.at[diag, c], m_s.at[2, c], m_r.at[2, c])
     project(diag)
 
-    for h in range(HL):
-        q = proj[:, :, h * HD : h * HD + HD].reshape(rows, HD)
-        qsend[h] = jnp.concatenate([q[:half], q[half:]], axis=-1).astype(BF16)
-    for d in range(1, HL):
-        hp = (h0 + d) % HL
-        send(qsend.at[hp], qrecv.at[h0], q_s.at[d], q_r.at[d], (zs[d], t))
+    ship(1)
     own_q = pltpu.make_async_copy(qsend.at[h0], qrecv.at[h0], l_s.at[3])
     own_q.start()
-    for h in range(HL):
-        k = proj[:, :, 256 + h * HD : 256 + h * HD + HD].reshape(rows, HD)
-        v = proj[:, :, 512 + h * HD : 512 + h * HD + HD].reshape(rows, HD)
-        kvsend[h] = jnp.concatenate([k, v], axis=-1).astype(BF16)
-    for e in range(1, G):
-        send(kvsend.at[h0], kv.at[s], f_s.at[0, e], f_r.at[0, e], (groups[e], t))
     own_kv = pltpu.make_async_copy(kvsend.at[h0], kv.at[s], l_s.at[4])
     own_kv.start()
-    for d in range(1, HL):
-        hp = (h0 + d) % HL
-        send(kvsend.at[hp], kv.at[s], k_s.at[d], k_r.at[d], (zs[d], t))
     send(wout, wf.at[t], w_s.at[0], w_r.at[0], (s, core))
 
     def unpack(h):
-        value = qrecv[h]
+        value = qrecv[h].astype(F32).reshape(half, 128).astype(BF16)
         zeros = jnp.zeros((half, HD), BF16)
         qpad[h * 2] = jnp.concatenate([value[:, :HD], zeros], axis=-1)
         qpad[h * 2 + 1] = jnp.concatenate([value[:, HD:], zeros], axis=-1)
@@ -139,7 +177,8 @@
     own_q.wait()
     unpack(h0)
     for d in range(1, HL):
-        arrive(qrecv.at[back[d]], q_s.at[d], q_r.at[d])
+        for p in range(2):
+            arrive(qrecv.at[back[d], (t // 2 + p) % 2], q_s.at[d, p], q_r.at[d, p])
         unpack(back[d])
     own_kv.wait()
 
@@ -200,7 +239,9 @@
 
     def group_arrives(d):
         for e in range(1, G):
-            arrive(kv.at[back[d] * G + (g + G - e) % G], f_s.at[d, e], f_r.at[d, e])
+            for p in range(2):
+                slot = kv.at[back[d] * G + (g + G - e) % G, (t // 2 + p) % 2]
+                arrive(slot, f_s.at[d, e, p], f_r.at[d, e, p])
 
     def emit(h):
         parts = []
@@ -209,22 +250,22 @@
             a = o[:, HD:] / o[:, :HD]
             for j in range(2):
                 b = a[j * block : (j + 1) * block]
-                asend[h * T + i * 2 + j] = jnp.concatenate(
+                asend[h * T + j * 2 + i] = jnp.concatenate(
                     [b[0:80], b[block - 80 : block]], axis=-1
                 ).astype(BF16)
 
     mine = t * HL + h0
     group_arrives(0)
+    pass_on(1, 0)
     for d in range(HL - 1):
         absorb(d, h0, HL // 2)
-        slot = kv.at[back[d + 1] * G + g]
-        arrive(slot, k_s.at[d + 1], k_r.at[d + 1])
-        for e in range(1, G):
-            send(slot, slot, f_s.at[d + 1, e], f_r.at[d + 1, e], (groups[e], t))
+        pass_on(d + 1, 1)
         if d == 0:
             arrive(wf.at[across], w_s.at[1], w_r.at[1])
             send(wf.at[across], wf.at[across], w_s.at[2], w_r.at[2], (s, core))
         absorb(d, h0 + HL // 2, HL // 2)
+        if d + 2 < HL:
+            pass_on(d + 2, 0)
         group_arrives(d + 1)
     for i in range(HL):
         d = (i + 1) % HL
@@ -260,12 +301,14 @@
     )
     updated = (tok[...].astype(F32) + gate[...] * mixed).astype(BF16)
     upd_out[...] = updated
-    fin[t] = (rms_normalize(updated.astype(F32)) * gain[...]).astype(BF16)
-    send(fin.at[t], fin.at[t], n_s.at[1], n_r.at[1], (s, across))
-    send(fin.at[t], fin.at[t], n_s.at[0], n_r.at[0], (s, core))
+    keep(fin, (rms_normalize(updated.astype(F32)) * gain[...]).astype(BF16))
+    for c in range(2):
+        send(fin.at[t, c], fin.at[t, c], n_s.at[1, c], n_r.at[1, c], (s, across))
+    for c in range(2):
+        send(fin.at[t, c], fin.at[t, c], n_s.at[0, c], n_r.at[0, c], (s, core))
 
     def heads(i, dst):
-        f = fin[i]
+        f = whole(fin, i)
         for k in range(2):
             hid = jnp.dot(f, w1v[k], preferred_element_type=F32) + b1[k : k + 1].astype(F32)
             hid = jax.nn.gelu(hid).astype(BF16)
@@ -275,14 +318,18 @@
 
     load_1.wait()
     heads(t, rrecv.at[t])
-    arrive(fin.at[core], n_s.at[0], n_r.at[0])
+    for c in range(2):
+        arrive(fin.at[core, c], n_s.at[0, c], n_r.at[0, c])
     heads(core, rsend.at[0])
     send(rsend.at[0], rrecv.at[t], r_s.at[0], r_r.at[0], (s, core))
-    arrive(fin.at[across], n_s.at[1], n_r.at[1])
-    send(fin.at[across], fin.at[across], n_s.at[2], n_r.at[2], (s, core))
+    for c in range(2):
+        slot = fin.at[across, c]
+        arrive(slot, n_s.at[1, c], n_r.at[1, c])
+        send(slot, slot, n_s.at[2, c], n_r.at[2, c], (s, core))
     heads(across, rsend.at[1])
     send(rsend.at[1], rrecv.at[t], r_s.at[1], r_r.at[1], (s, across))
-    arrive(fin.at[diag], n_s.at[2], n_r.at[2])
+    for c in range(2):
+        arrive(fin.at[diag, c], n_s.at[2, c], n_r.at[2, c])
     heads(diag, rsend.at[2])
     send(rsend.at[2], rrecv.at[t], r_s.at[2], r_r.at[2], (s, diag))
     for i, peer in enumerate((core, across, diag)):
@@ -320,18 +367,26 @@
             jax.ShapeDtypeStruct((block, D), BF16),
             jax.ShapeDtypeStruct((16, block), F32),
         ),
-        in_specs=[VM, VM, HB, HB, VM, VM, VM, HB, VM, VM],
+        in_specs=[HB] * 10,
         out_specs=(VM, VM),
         scratch_shapes=[
+            pltpu.VMEM((block, D), BF16),
+            pltpu.VMEM((2, D), F32),
+            pltpu.VMEM((1, D), F32),
+            pltpu.VMEM((1, D), F32),
+            pltpu.VMEM((1, block), jnp.int32),
+            pltpu.VMEM(head_b1.shape, BF16),
+            pltpu.VMEM((head_w2.shape[0], head_w2.shape[2], head_w2.shape[1]), BF16),
+            dma((7,)),
             pltpu.VMEM(w_qkv.shape, BF16),
             pltpu.VMEM((T, width, D), BF16),
             pltpu.VMEM(head_w1.shape, BF16),
-            pltpu.VMEM((T, block, D), BF16),
+            pltpu.VMEM((T, 2, block, D // 2), BF16),
             pltpu.VMEM((T, block, 3 * width), F32),
-            pltpu.VMEM((HL, half, 128), BF16),
-            pltpu.VMEM((HL, rows, 128), BF16),
-            pltpu.VMEM((HL, half, 128), BF16),
-            pltpu.VMEM((S, rows, 128), BF16),
+            pltpu.VMEM((HL, 2, block, 128), BF16),
+            pltpu.VMEM((HL, 2, half, 128), BF16),
+            pltpu.VMEM((HL, 2, block, 128), BF16),
+            pltpu.VMEM((S, 2, half, 128), BF16),
             pltpu.VMEM((2 * HL, half, 128), BF16),
             pltpu.VMEM((per * rows, 128), BF16),
             pltpu.VMEM((2 * HL, half, 128), F32),
@@ -339,16 +394,16 @@
             pltpu.VMEM((N, 80, 128), BF16),
             pltpu.VMEM((N, 80, 128), BF16),
             pltpu.VMEM((block, D), BF16),
-            pltpu.VMEM((T, block, D), BF16),
+            pltpu.VMEM((T, 2, block, D // 2), BF16),
             pltpu.VMEM((3, 32, block), F32),
             pltpu.VMEM((T, 32, block), F32),
-            dma((3,)), dma((3,)), dma((3,)), dma((3,)),
-            dma((HL,)), dma((HL,)), dma((HL,)), dma((HL,)),
-            dma((HL, G)), dma((HL, G)), dma((HL, T)), dma((HL, T)),
-            dma((3,)), dma((3,)), dma((3,)), dma((3,)), dma((6,)),
+            dma((3, 2)), dma((3, 2)), dma((3,)), dma((3,)),
+            dma((HL, 2)), dma((HL, 2)), dma((HL, 2)), dma((HL, 2)),
+            dma((HL, G, 2)), dma((HL, G, 2)), dma((HL, T)), dma((HL, T)),
+            dma((3, 2)), dma((3, 2)), dma((3,)), dma((3,)), dma((6,)),
         ],
         compiler_params=pltpu.CompilerParams(
-            collective_id=0, has_side_effects=True, vmem_limit_bytes=48 * 2**20
+            collective_id=0, has_side_effects=True, vmem_limit_bytes=63 * 2**20
         ),
         name="sublayer",
     )(

time: 84.7 us -> 72.1 us (0.85)
  Pallas kernels: 74.6 us -> 68.2 us
  local copies, waits for them, and re-layouts: 8.99 us -> 3.01 us
    pallas_call x1, Pallas kernels: 74.6 us -> 68.2 us  [body(): pl.pallas_call(functools.partial(kernel, S, HL, T), out_shape=(jax.ShapeD...]
    unnamed x20 -> x2, local copies, waits for them, and re-layouts: 8.99 us -> 3.01 us
where the time goes in v3:
time: 72.1 us; the launch traced here: 71.9 us
  Pallas kernels  68.2 us (95%)
  local copies, waits for them, and re-layouts  3.01 us (4%)
    pallas_call x1, Pallas kernels, body(): pl.pallas_call(functools.partial(kernel, S, HL, T), out_shape=(jax.ShapeD...  68.2 us
    unnamed x2, local copies, waits for them, and re-layouts  3.01 us

profile of v3, /device:TPU:0, one launch (start us, length us, event | category | flops | bytes accessed | tf_op | source)
XLA Modules:
  0.0 71.9 jit_solution(779886078049949458)
XLA Ops:
  0.6 68.2 %sublayer.1 = (bf16[136,1024]{1,0:T(8,128)(2,1)}, f32[16,136]{1,0:T(8,128)}) custom-call(bf16[136,1024]{1,0:T(8,128)(2,1)} %tok_h.1, f32[2,1024]{1,0:T(2,128)} %ss_h.1, bf16[3,1024,256]{2,1,0:T(8,128)(2,1)} %wqkv.1, bf16[256,1024]{1,0:T(8,128)(2,1)} %wout.1, f32[1,1024]{1,0:T(1,128)} %bitcast.7, f32[1,1024]{1,0:T(1,128)} %bitcast.8, s32[1,136]{1,0:T(1,128)} %bitcast.9, ...), custom_call_target="tpu_custom_call" | custom-call | tf_op jit(solution)/shard_map/sublayer/pallas_call | solution.py:364
  68.9 1.7 %copy.14 = bf16[136,1024]{1,0:T(8,128)(2,1)} copy(bf16[136,1024]{1,0:T(8,128)(2,1)} %get-tuple-element.8) | data formatting | bytes 557056
  70.5 1.3 %copy.15 = f32[136,16]{0,1:T(8,128)} copy(f32[136,16]{0,1:T(8,128)} %bitcast.6) | data formatting | bytes 17408
